TPU v7x, 256 devices: a whole 4x4x8 slice. The times are simulated.
256 devices in a mesh: wa: 8 (over z), vert: 32 (over y, x, core).
Axes of the slice: x: 4, y: 4, z: 8, core: 2. Of those that a mesh axis runs over, the one named last changes fastest.
Arguments:
- hidden_in: bfloat16 [384, 8192], P(None, 'wa')
- gate_levels: bfloat16 [8192, 28672], P('wa', 'vert'), may hold values from -127 to 127, as said below
- up_levels: bfloat16 [8192, 28672], P('wa', 'vert'), may hold values from -127 to 127, as said below
- gate_scale: float32 [28672], P('vert'), as said below
- up_scale: float32 [28672], P('vert'), as said below
- down_levels: bfloat16 [28672, 8192], P('vert', 'wa'), may hold values from -127 to 127, as said below
- down_scale: float32 [8192], P('wa'), as said below
- norm_gain: float32 [8192], P('wa'), may hold values from 0.5 to 1.5
- head_weight: bfloat16 [8192, 16000], P('wa', 'vert')
- reward_states: bfloat16 [8, 384, 4096], P('wa', None, 'vert'), may hold values from -6 to 6
- reward_gain: float32 [8, 4096], P('wa'), may hold values from 0.5 to 1.5
- reward_heads: bfloat16 [8, 4096, 16000], P('wa', None, 'vert')
- preference: int32 [384, 8], P(None, 'wa'), may hold values from 0 to 16
- token_ids: int32 [384], P('wa'), may hold values from 0 to 15999
Outputs:
- log_probs: float32 [384, 16000], P('wa', 'vert')
- chosen: float32 [384], P('wa')
Inputs may be any that keep to these rules, and one draw needn't show every extreme that they name: `gate_levels`: whole numbers. `up_levels`: whole numbers. `down_levels`: whole numbers. `gate_scale`: positive. `up_scale`: positive. `down_scale`: positive.
All inputs are finite; a program needn't handle non-finite values.
Results may differ from a plain program's by a relative error of at most 0.0025.
Values may be sent and summed in bfloat16 or wider, within the bound.
No kernel may reach another device: no remote copies, remote signals or barrier semaphores. Data moves between devices by JAX's collectives and lax.ppermute only.
A program may use at most 64 MiB of HBM per device.

v0:
```python
import jax
import jax.numpy as jnp
from jax import lax
from jax.sharding import PartitionSpec as P

D = 8192


def log_total(values):
    local_top = jnp.max(values, axis=-1)
    top = lax.pmax(local_top, "vert")
    total = lax.psum(jnp.sum(jnp.exp(values - top[..., None]), axis=-1), "vert")
    return top + jnp.log(total)


def normalize(resid, norm_gain):
    squares = lax.psum(jnp.sum(resid * resid, axis=1), "wa")
    return (resid * lax.rsqrt(squares[:, None] / D + 1e-05) * norm_gain).astype(jnp.bfloat16)


def local(
    hidden_in,
    gate_levels,
    up_levels,
    gate_scale,
    up_scale,
    down_levels,
    down_scale,
    norm_gain,
    head_weight,
    reward_states,
    reward_gain,
    reward_heads,
    preference,
    token_ids,
):
    gate_part = jnp.dot(hidden_in, gate_levels, preferred_element_type=jnp.float32)
    up_part = jnp.dot(hidden_in, up_levels, preferred_element_type=jnp.float32)
    gate, up = lax.psum((gate_part, up_part), "wa")
    hidden = (jax.nn.silu(gate * gate_scale) * (up * up_scale)).astype(jnp.bfloat16)
    down_part = jnp.dot(hidden, down_levels, preferred_element_type=jnp.float32)
    down = lax.psum(down_part, "vert") * down_scale
    resid = hidden_in.astype(jnp.float32) + down
    normed = normalize(resid, norm_gain)
    base_part = jnp.dot(normed, head_weight, preferred_element_type=jnp.float32)
    states = lax.all_gather(reward_states, "vert", axis=2, tiled=True)
    state_values = states.astype(jnp.float32)
    state_scale = lax.rsqrt(jnp.mean(state_values * state_values, axis=2, keepdims=True) + 1e-05)
    reward_normed = (state_values * state_scale * reward_gain[:, None, :]).astype(jnp.bfloat16)
    reward_logits = jnp.einsum(
        "rnd,rdv->rnv", reward_normed, reward_heads, preferred_element_type=jnp.float32
    )
    reward_logp = reward_logits - log_total(reward_logits)[..., None]
    weights = preference.astype(jnp.float32).T / 16.0
    weighted = jnp.sum(weights[:, :, None] * reward_logp, axis=0)
    base_rows, reward_rows = (
        lax.psum_scatter(base_part, "wa", scatter_dimension=0, tiled=True),
        lax.psum_scatter(weighted, "wa", scatter_dimension=0, tiled=True),
    )
    base_logp = base_rows - log_total(base_rows)[:, None]
    mix = base_logp + reward_rows
    log_probs = mix - log_total(mix)[:, None]
    columns = log_probs.shape[1]
    vocab_index = lax.axis_index("vert") * columns + lax.iota(jnp.int32, columns)
    picked = jnp.sum(jnp.where(vocab_index[None, :] == token_ids[:, None], log_probs, 0.0), axis=1)
    chosen = lax.psum(picked, "vert")
    return (log_probs, chosen)


def solution(mesh):
    return jax.shard_map(
        local,
        mesh=mesh,
        in_specs=(
            P(None, "wa"),
            P("wa", "vert"),
            P("wa", "vert"),
            P("vert"),
            P("vert"),
            P("vert", "wa"),
            P("wa"),
            P("wa"),
            P("wa", "vert"),
            P("wa", None, "vert"),
            P("wa", None),
            P("wa", None, "vert"),
            P(None, "wa"),
            P("wa"),
        ),
        out_specs=(P("wa", "vert"), P("wa")),
        check_vma=False,
    )
```

profile of v0, /device:TPU:1, one launch (start us, length us, event | category | flops | bytes accessed | tf_op | source)
XLA Modules:
  0.0 702.5 jit_solution(15787238454085852242)
XLA Ops:
  7.2 0.0 copy-start
  7.2 0.0 copy-start.3
  7.2 0.0 all-reduce.8.cloned.1.call-start
  7.2 0.0 copy-start.10
  7.2 3.9 fusion.17
  11.2 0.0 copy-done.3
  11.2 0.0 copy-done.10
  11.2 2.0 fusion.18
  13.2 0.0 copy-start.13
  13.2 0.0 all-reduce.8.cloned.1.call-update
  13.3 0.0 all-reduce.6.cloned.1.call-start
  13.3 89.1 %all-reduce.8.cloned.1.call-done = (f32[384,896]{1,0:T(8,128)}, f32[384,896]{1,0:T(8,128)}) async-done(((f32[384,896]{1,0:T(8,128)}, f32[384,896]{1,0:T(8,128)}), (f32[384,896]{1,0:T(8,128)}, f32[384,896]{1,0:T(8,128)})) %all-reduce.8.cloned.1.call-update) | async-done | bytes 2752528 | tf_op jit(solution)/shard_map/psum | solution.py:39
  102.5 0.0 copy-done
  102.5 0.0 copy-done.12
  102.5 0.0 copy-done.13
  102.5 3.9 fusion.13
  106.4 0.0 copy-start.6
  106.4 0.0 all-reduce.6.cloned.1.call-update
  106.4 0.0 copy-start.7
  106.5 0.0 reduce-scatter.7.cloned.1.call-start
  106.5 116.9 %all-reduce.6.cloned.1.call-done = f32[384,1024]{1,0:T(8,128)} async-done(((f32[384,1024]{1,0:T(8,128)}), f32[384,1024]{1,0:T(8,128)}) %all-reduce.6.cloned.1.call-update) | async-done | bytes 1572880 | tf_op jit(solution)/shard_map/psum | solution.py:42
  223.4 0.0 copy-done.6
  223.4 2.1 multiply_reduce_fusion
  225.4 13.7 %psum.59 = f32[384]{0:T(512)S(1)} all-reduce(f32[384]{0:T(512)S(1)} %multiply_reduce_fusion), channel_id=1, replica_groups=mesh['wa'=8,'vert'=32] {'wa'}, use_global_device_ids=true, to_apply=%region_4.5 | all-reduce | flops 384 | bytes 3072 | tf_op jit(solution)/shard_map/psum | solution.py:17
  239.1 0.0 copy-done.7
  239.1 0.0 copy-done.1
  239.1 0.0 copy-start.8
  239.1 3.0 fusion.9
  242.1 0.0 reduce-scatter.7.cloned.1.call-update
  242.1 0.0 all-gather.2.cloned.1.call-start
  242.2 0.5 all-gather.2.cloned.1.call-update
  242.7 0.0 reduce-scatter.9.cloned.1.call-start
  242.8 0.0 copy-done.8
  242.8 33.5 %reduce-scatter.7.cloned.1.call-done = f32[48,500]{1,0:T(8,128)} async-done(((f32[384,500]{1,0:T(8,128)}), f32[48,500]{1,0:T(8,128)}) %reduce-scatter.7.cloned.1.call-update) | async-done | bytes 96016
  276.3 1.0 copy.23
  277.3 0.0 copy-start.4
  277.4 0.0 copy-start.11
  277.4 1.1 reduce_max.29
  278.5 55.9 %all-gather.2.cloned.1.call-done = bf16[1,384,4096]{2,1,0:T(8,128)(2,1)} async-done(((bf16[1,384,128]{2,1,0:T(8,128)(2,1)}), bf16[1,384,4096]{2,1,0:T(8,128)(2,1)}) %all-gather.2.cloned.1.call-update) | async-done | bytes 3145744 | tf_op jit(solution)/shard_map/all_gather | solution.py:46
  334.3 2.7 fusion
  337.1 0.0 copy-done.11
  337.1 0.1 copy-done.2
  337.2 4.6 fusion.16
  341.8 62.3 %all-reduce.1 = (f32[1,384]{1,0:T(1,128)S(1)}, f32[48]{0:T(128)S(1)}) all-reduce(f32[1,384]{1,0:T(1,128)S(1)} %reduce_max.31, f32[48]{0:T(128)S(1)} %reduce_max.29), channel_id=1, replica_groups=mesh['wa'=8,'vert'=32] {'vert'}, use_global_device_ids=true, to_apply=%region_12.13 | all-reduce | flops 432 | bytes 3456 | tf_op jit(solution)/shard_map/pmax | solution.py:11
  404.1 0.2 exponential_reduce_fusion
  404.3 0.0 copy-done.4
  404.3 0.1 exponential_reduce_fusion.2
  404.4 65.2 %all-reduce = (f32[1,384]{1,0:T(1,128)S(1)}, f32[48]{0:T(128)S(1)}) all-reduce(f32[1,384]{1,0:T(1,128)S(1)} %reduce_sum.64, f32[48]{0:T(128)S(1)} %exponential_reduce_fusion.2), channel_id=1, replica_groups=mesh['wa'=8,'vert'=32] {'vert'}, use_global_device_ids=true, to_apply=%region_14.15 | all-reduce | flops 432 | bytes 3456 | tf_op jit(solution)/shard_map/psum | solution.py:12
  469.6 0.1 subtract_multiply_fusion
  469.7 0.0 copy-start.5
  469.7 0.0 copy-start.9
  469.7 1.2 copy.24
  470.9 0.0 reduce-scatter.9.cloned.1.call-update
  471.0 29.6 %reduce-scatter.9.cloned.1.call-done = f32[48,500]{1,0:T(8,128)} async-done(((f32[384,500]{1,0:T(8,128)}), f32[48,500]{1,0:T(8,128)}) %reduce-scatter.9.cloned.1.call-update) | async-done | bytes 96016
  500.5 1.0 copy.25
  501.6 0.0 copy-done.5
  501.6 0.1 fusion.15
  501.7 67.5 %pmax.23 = f32[48]{0:T(128)S(1)} all-reduce(f32[48]{0:T(128)S(1)} %get-tuple-element.14), channel_id=1, replica_groups=mesh['wa'=8,'vert'=32] {'vert'}, use_global_device_ids=true, to_apply=%region_17.18 | all-reduce | flops 48 | bytes 384 | tf_op jit(solution)/shard_map/pmax | solution.py:11
  569.2 0.1 exponential_reduce_fusion.1
  569.3 62.7 %psum.62 = f32[48]{0:T(128)S(1)} all-reduce(f32[48]{0:T(128)S(1)} %exponential_reduce_fusion.1), channel_id=1, replica_groups=mesh['wa'=8,'vert'=32] {'vert'}, use_global_device_ids=true, to_apply=%region_19.20 | all-reduce | flops 48 | bytes 384 | tf_op jit(solution)/shard_map/psum | solution.py:12
  631.9 0.0 copy-done.9
  632.0 0.2 select_reduce_fusion
  632.1 0.8 copy.20
  632.9 63.2 %psum.63 = f32[48]{0:T(128)} all-reduce(f32[48]{0:T(128)S(1)} %get-tuple-element.12), channel_id=1, replica_groups=mesh['wa'=8,'vert'=32] {'vert'}, use_global_device_ids=true, to_apply=%region_21.22 | all-reduce | flops 48 | bytes 384 | tf_op jit(solution)/shard_map/psum | solution.py:66
  (13 shorter events, 0.1 us)
Async XLA Ops:
  7.2 95.3 %copy-start = (bf16[896,1024]{1,0:T(8,128)(2,1)S(1)}, bf16[896,1024]{1,0:T(8,128)(2,1)}, u32[]{:S(2)}) copy-start(bf16[896,1024]{1,0:T(8,128)(2,1)} %param.19) | copy-start | bytes 5505028
  7.2 4.0 copy-start.3
  7.2 95.3 %all-reduce.8.cloned.1.call-start = ((), (), s32[]{:S(2)}) async-start(), calls=%async_computation.6 | async-start | bytes 5505024 | tf_op jit(solution)/shard_map/psum | solution.py:39
  7.2 4.0 copy-start.10
  13.2 89.2 %copy-start.12 = (f32[896]{0:T(1024)S(1)}, f32[896]{0:T(1024)}, u32[]{:S(2)}) copy-start(f32[896]{0:T(1024)} %param.18) | copy-start | bytes 10756
  13.2 89.2 %copy-start.13 = (f32[896]{0:T(1024)S(1)}, f32[896]{0:T(1024)}, u32[]{:S(2)}) copy-start(f32[896]{0:T(1024)} %param.17) | copy-start | bytes 10756
  13.3 210.1 %all-reduce.6.cloned.1.call-start = ((), (), s32[]{:S(2)}) async-start(), calls=%async_computation.2 | async-start | bytes 3145728 | tf_op jit(solution)/shard_map/psum | solution.py:42
  106.4 116.9 %copy-start.6 = (f32[1024]{0:T(1024)S(1)}, f32[1024]{0:T(1024)}, u32[]{:S(2)}) copy-start(f32[1024]{0:T(1024)} %param.20) | copy-start | bytes 12292
  106.4 132.7 %copy-start.7 = (f32[1024]{0:T(1024)S(1)}, f32[1024]{0:T(1024)}, u32[]{:S(2)}) copy-start(f32[1024]{0:T(1024)} %param.21) | copy-start | bytes 12292
  106.5 169.9 %reduce-scatter.7.cloned.1.call-start = ((), (), s32[]{:S(2)}) async-start(), calls=%async_computation.4 | async-start | bytes 884736
  223.4 15.8 %copy-start.1 = (f32[384,1024]{1,0:T(8,128)S(1)}, f32[384,1024]{1,0:T(8,128)}, u32[]{:S(2)}) copy-start(f32[384,1024]{1,0:T(8,128)} %all-reduce.6.cloned.1.call-done) | copy-start | bytes 4718596
  239.1 3.6 copy-start.8
  242.1 92.2 %all-gather.2.cloned.1.call-start = ((), (), s32[]{:S(2)}) async-start(), calls=%async_computation.3 | async-start | bytes 3244032 | tf_op jit(solution)/shard_map/all_gather | solution.py:46
  242.7 257.8 %reduce-scatter.9.cloned.1.call-start = ((), (), s32[]{:S(2)}) async-start(), calls=%async_computation.5 | async-start | bytes 884736
  277.3 126.9 %copy-start.4 = (f32[48,500]{0,1:T(8,128)}, f32[48,500]{0,1:T(8,128)S(1)}, u32[]{:S(2)}) copy-start(f32[48,500]{0,1:T(8,128)S(1)} %copy.23) | copy-start | bytes 288004
  277.4 59.7 %copy-start.11 = (f32[1,4096]{1,0:T(1,128)S(1)}, f32[1,4096]{1,0:T(1,128)}, u32[]{:S(2)}) copy-start(f32[1,4096]{1,0:T(1,128)} %param.24) | copy-start | bytes 49156
  334.3 2.8 copy-start.2
  469.7 31.8 %copy-start.5 = (f32[48,500]{0,1:T(8,128)S(1)}, f32[48,500]{0,1:T(8,128)}, u32[]{:S(2)}) copy-start(f32[48,500]{0,1:T(8,128)} %copy-done.4) | copy-start | bytes 288004
  469.7 162.2 %copy-start.9 = (s32[48]{0:T(128)S(1)}, s32[48]{0:T(128)}, u32[]{:S(2)}) copy-start(s32[48]{0:T(128)} %param.27) | copy-start | bytes 580
Sparse Core Ops, SparseCore 0:
  13.4 89.0 all-reduce.7
  106.6 116.7 all-reduce.5
  242.3 34.0 reduce-scatter.6
  279.0 55.3 all-gather.1
  471.1 29.4 reduce-scatter.8
where the time goes:
time: 703 us
  blocking collectives  335 us (48%)
  waiting for transfers between devices  326 us (46%)
  matrix products  17.5 us (2%)
  between operations  13.9 us (2%)
    pmax x2, blocking collectives, log_total(): top = lax.pmax(local_top, 'vert')  130 us
    psum x2, blocking collectives, log_total(): total = lax.psum(jnp.sum(jnp.exp(values - top[..., None]), axis=-1), 'vert')  128 us
    psum x1, waiting for transfers between devices, local(): down = lax.psum(down_part, 'vert') * down_scale  117 us
    psum x1, waiting for transfers between devices, local(): gate, up = lax.psum((gate_part, up_part), 'wa')  89.1 us
    unnamed x7, waiting for transfers between devices  63.7 us
    psum x1, blocking collectives, local(): chosen = lax.psum(picked, 'vert')  63.2 us
    all_gather x1, waiting for transfers between devices, local(): states = lax.all_gather(reward_states, 'vert', axis=2, tiled=True)  55.9 us
  transfers between devices with their start and end apart: 5, of which 5 were waited for; matrix products, arithmetic and copies ran while one was open for 0% of the time, Pallas kernels for 0%

commit v1 on v0

--- a/solution.py
+++ b/solution.py
@@ -4,6 +4,14 @@
 from jax.sharding import PartitionSpec as P
 
 D = 8192
+
+
+def added_up(x, axis):
+    size, acc = (lax.axis_size(axis), x)
+    for far in [1 << k for k in range(size.bit_length() - 1)]:
+        swap = [(i, i ^ far) for i in range(size)]
+        acc = acc + lax.ppermute(acc, axis, swap)
+    return acc
 
 
 def log_total(values):
@@ -63,7 +71,7 @@
     columns = log_probs.shape[1]
     vocab_index = lax.axis_index("vert") * columns + lax.iota(jnp.int32, columns)
     picked = jnp.sum(jnp.where(vocab_index[None, :] == token_ids[:, None], log_probs, 0.0), axis=1)
-    chosen = lax.psum(picked, "vert")
+    chosen = added_up(picked, "vert")
     return (log_probs, chosen)
 
 

time: 703 us -> 656 us (0.933)
  blocking collectives: 335 us -> 271 us
  waiting for transfers between devices: 326 us -> 338 us
    psum x1 -> x0, blocking collectives: 63.2 us -> none  [local(): chosen = lax.psum(picked, 'vert')]
    ppermute x0 -> x5, waiting for transfers between devices: none -> 12.6 us  [added_up(): acc = acc + lax.ppermute(acc, axis, swap)]
  transfers between devices with their start and end apart: 5 -> 10, of which waited for: 5 -> 10; matrix products, arithmetic and copies ran while one was open for 0% -> 0% of each run, Pallas kernels for 0% -> 0%
where the time goes in v1:
time: 656 us; the launch traced here: 653 us
  waiting for transfers between devices  338 us (52%)
  blocking collectives  271 us (41%)
  matrix products  17.5 us (3%)
  between operations  14 us (2%)
  other arithmetic  7.18 us (1%)
    pmax x2, blocking collectives, log_total(): top = lax.pmax(local_top, 'vert')  130 us
    psum x2, blocking collectives, log_total(): total = lax.psum(jnp.sum(jnp.exp(values - top[..., None]), axis=-1), 'vert')  128 us
    psum x1, waiting for transfers between devices, local(): down = lax.psum(down_part, 'vert') * down_scale  117 us
    psum x1, waiting for transfers between devices, local(): gate, up = lax.psum((gate_part, up_part), 'wa')  89.1 us
    unnamed x7, waiting for transfers between devices  63.7 us
    all_gather x1, waiting for transfers between devices, local(): states = lax.all_gather(reward_states, 'vert', axis=2, tiled=True)  55.9 us
    psum x1, blocking collectives, normalize(): squares = lax.psum(jnp.sum(resid * resid, axis=1), 'wa')  13.7 us
  transfers between devices with their start and end apart: 10, of which 10 were waited for; matrix products, arithmetic and copies ran while one was open for 0% of the time, Pallas kernels for 0%

profile of v1, /device:TPU:1, one launch (start us, length us, event | category | flops | bytes accessed | tf_op | source)
XLA Modules:
  0.0 653.3 jit_solution(2875951833987203796)
XLA Ops:
  7.2 0.0 copy-start
  7.2 0.0 copy-start.3
  7.2 0.0 all-reduce.8.cloned.1.call-start
  7.2 0.0 copy-start.10
  7.2 3.9 fusion.17
  11.2 0.0 copy-done.3
  11.2 0.0 copy-done.10
  11.2 2.0 fusion.18
  13.2 0.0 all-reduce.8.cloned.1.call-update
  13.3 0.0 all-reduce.6.cloned.1.call-start
  13.3 89.1 %all-reduce.8.cloned.1.call-done = (f32[384,896]{1,0:T(8,128)}, f32[384,896]{1,0:T(8,128)}) async-done(((f32[384,896]{1,0:T(8,128)}, f32[384,896]{1,0:T(8,128)}), (f32[384,896]{1,0:T(8,128)}, f32[384,896]{1,0:T(8,128)})) %all-reduce.8.cloned.1.call-update) | async-done | bytes 2752528 | tf_op jit(solution)/shard_map/psum | solution.py:47
  102.5 0.0 copy-done
  102.5 0.0 copy-done.12
  102.5 0.0 copy-done.13
  102.5 3.9 fusion.13
  106.4 0.0 all-reduce.6.cloned.1.call-update
  106.4 0.0 copy-start.7
  106.5 0.0 reduce-scatter.7.cloned.1.call-start
  106.5 116.9 %all-reduce.6.cloned.1.call-done = f32[384,1024]{1,0:T(8,128)} async-done(((f32[384,1024]{1,0:T(8,128)}), f32[384,1024]{1,0:T(8,128)}) %all-reduce.6.cloned.1.call-update) | async-done | bytes 1572880 | tf_op jit(solution)/shard_map/psum | solution.py:50
  223.4 2.1 multiply_reduce_fusion
  225.4 13.7 %psum.52 = f32[384]{0:T(512)S(1)} all-reduce(f32[384]{0:T(512)S(1)} %multiply_reduce_fusion), channel_id=1, replica_groups=mesh['wa'=8,'vert'=32] {'wa'}, use_global_device_ids=true, to_apply=%region_4.5 | all-reduce | flops 384 | bytes 3072 | tf_op jit(solution)/shard_map/psum | solution.py:25
  239.1 0.0 copy-done.1
  239.1 0.0 copy-start.8
  239.1 3.0 fusion.9
  242.1 0.0 reduce-scatter.7.cloned.1.call-update
  242.1 0.0 all-gather.2.cloned.1.call-start
  242.2 0.5 all-gather.2.cloned.1.call-update
  242.7 0.0 reduce-scatter.9.cloned.1.call-start
  242.8 33.5 %reduce-scatter.7.cloned.1.call-done = f32[48,500]{1,0:T(8,128)} async-done(((f32[384,500]{1,0:T(8,128)}), f32[48,500]{1,0:T(8,128)}) %reduce-scatter.7.cloned.1.call-update) | async-done | bytes 96016
  276.3 1.0 copy.23
  277.4 0.0 copy-start.11
  277.4 1.1 reduce_max.29
  278.5 55.9 %all-gather.2.cloned.1.call-done = bf16[1,384,4096]{2,1,0:T(8,128)(2,1)} async-done(((bf16[1,384,128]{2,1,0:T(8,128)(2,1)}), bf16[1,384,4096]{2,1,0:T(8,128)(2,1)}) %all-gather.2.cloned.1.call-update) | async-done | bytes 3145744 | tf_op jit(solution)/shard_map/all_gather | solution.py:54
  334.3 2.7 fusion
  337.1 0.1 copy-done.2
  337.2 4.6 fusion.16
  341.8 62.3 %all-reduce.1 = (f32[1,384]{1,0:T(1,128)S(1)}, f32[48]{0:T(128)S(1)}) all-reduce(f32[1,384]{1,0:T(1,128)S(1)} %reduce_max.31, f32[48]{0:T(128)S(1)} %reduce_max.29), channel_id=1, replica_groups=mesh['wa'=8,'vert'=32] {'vert'}, use_global_device_ids=true, to_apply=%region_12.13 | all-reduce | flops 432 | bytes 3456 | tf_op jit(solution)/shard_map/pmax | solution.py:19
  404.1 0.2 exponential_reduce_fusion
  404.3 0.1 exponential_reduce_fusion.2
  404.4 65.2 %all-reduce = (f32[1,384]{1,0:T(1,128)S(1)}, f32[48]{0:T(128)S(1)}) all-reduce(f32[1,384]{1,0:T(1,128)S(1)} %reduce_sum.64, f32[48]{0:T(128)S(1)} %exponential_reduce_fusion.2), channel_id=1, replica_groups=mesh['wa'=8,'vert'=32] {'vert'}, use_global_device_ids=true, to_apply=%region_14.15 | all-reduce | flops 432 | bytes 3456 | tf_op jit(solution)/shard_map/psum | solution.py:20
  469.6 0.1 subtract_multiply_fusion
  469.7 0.0 copy-start.5
  469.7 0.0 copy-start.9
  469.7 1.2 copy.24
  470.9 0.0 reduce-scatter.9.cloned.1.call-update
  471.0 29.6 %reduce-scatter.9.cloned.1.call-done = f32[48,500]{1,0:T(8,128)} async-done(((f32[384,500]{1,0:T(8,128)}), f32[48,500]{1,0:T(8,128)}) %reduce-scatter.9.cloned.1.call-update) | async-done | bytes 96016
  500.5 1.0 copy.25
  501.6 0.1 fusion.15
  501.7 67.5 %pmax.23 = f32[48]{0:T(128)S(1)} all-reduce(f32[48]{0:T(128)S(1)} %get-tuple-element.14), channel_id=1, replica_groups=mesh['wa'=8,'vert'=32] {'vert'}, use_global_device_ids=true, to_apply=%region_17.18 | all-reduce | flops 48 | bytes 384 | tf_op jit(solution)/shard_map/pmax | solution.py:19
  569.2 0.1 exponential_reduce_fusion.1
  569.3 62.7 %psum.55 = f32[48]{0:T(128)S(1)} all-reduce(f32[48]{0:T(128)S(1)} %exponential_reduce_fusion.1), channel_id=1, replica_groups=mesh['wa'=8,'vert'=32] {'vert'}, use_global_device_ids=true, to_apply=%region_19.20 | all-reduce | flops 48 | bytes 384 | tf_op jit(solution)/shard_map/psum | solution.py:20
  632.0 0.2 select_reduce_fusion
  632.1 0.7 collective-permute-start
  632.8 0.8 collective-permute-done
  633.7 0.0 collective-permute-start.1
  633.7 2.4 collective-permute-done.1
  636.1 0.0 collective-permute-start.2
  636.1 3.9 collective-permute-done.2
  640.0 0.0 collective-permute-start.3
  640.0 2.4 collective-permute-done.3
  642.4 0.0 collective-permute-start.4
  642.4 0.8 copy.20
  643.1 3.1 collective-permute-done.4
  646.2 0.5 add.93
  (27 shorter events, 0.2 us)
Async XLA Ops:
  7.2 95.3 %copy-start = (bf16[896,1024]{1,0:T(8,128)(2,1)S(1)}, bf16[896,1024]{1,0:T(8,128)(2,1)}, u32[]{:S(2)}) copy-start(bf16[896,1024]{1,0:T(8,128)(2,1)} %param.19) | copy-start | bytes 5505028
  7.2 4.0 copy-start.3
  7.2 95.3 %all-reduce.8.cloned.1.call-start = ((), (), s32[]{:S(2)}) async-start(), calls=%async_computation.6 | async-start | bytes 5505024 | tf_op jit(solution)/shard_map/psum | solution.py:47
  7.2 4.0 copy-start.10
  13.2 89.2 %copy-start.12 = (f32[896]{0:T(1024)S(1)}, f32[896]{0:T(1024)}, u32[]{:S(2)}) copy-start(f32[896]{0:T(1024)} %param.18) | copy-start | bytes 10756
  13.2 89.2 %copy-start.13 = (f32[896]{0:T(1024)S(1)}, f32[896]{0:T(1024)}, u32[]{:S(2)}) copy-start(f32[896]{0:T(1024)} %param.17) | copy-start | bytes 10756
  13.3 210.1 %all-reduce.6.cloned.1.call-start = ((), (), s32[]{:S(2)}) async-start(), calls=%async_computation.2 | async-start | bytes 3145728 | tf_op jit(solution)/shard_map/psum | solution.py:50
  106.4 116.9 %copy-start.6 = (f32[1024]{0:T(1024)S(1)}, f32[1024]{0:T(1024)}, u32[]{:S(2)}) copy-start(f32[1024]{0:T(1024)} %param.20) | copy-start | bytes 12292
  106.4 132.7 %copy-start.7 = (f32[1024]{0:T(1024)S(1)}, f32[1024]{0:T(1024)}, u32[]{:S(2)}) copy-start(f32[1024]{0:T(1024)} %param.21) | copy-start | bytes 12292
  106.5 169.9 %reduce-scatter.7.cloned.1.call-start = ((), (), s32[]{:S(2)}) async-start(), calls=%async_computation.4 | async-start | bytes 884736
  223.4 15.8 %copy-start.1 = (f32[384,1024]{1,0:T(8,128)S(1)}, f32[384,1024]{1,0:T(8,128)}, u32[]{:S(2)}) copy-start(f32[384,1024]{1,0:T(8,128)} %all-reduce.6.cloned.1.call-done) | copy-start | bytes 4718596
  239.1 3.6 copy-start.8
  242.1 92.2 %all-gather.2.cloned.1.call-start = ((), (), s32[]{:S(2)}) async-start(), calls=%async_computation.3 | async-start | bytes 3244032 | tf_op jit(solution)/shard_map/all_gather | solution.py:54
  242.7 257.8 %reduce-scatter.9.cloned.1.call-start = ((), (), s32[]{:S(2)}) async-start(), calls=%async_computation.5 | async-start | bytes 884736
  277.3 126.9 %copy-start.4 = (f32[48,500]{0,1:T(8,128)}, f32[48,500]{0,1:T(8,128)S(1)}, u32[]{:S(2)}) copy-start(f32[48,500]{0,1:T(8,128)S(1)} %copy.23) | copy-start | bytes 288004
  277.4 59.7 %copy-start.11 = (f32[1,4096]{1,0:T(1,128)S(1)}, f32[1,4096]{1,0:T(1,128)}, u32[]{:S(2)}) copy-start(f32[1,4096]{1,0:T(1,128)} %param.24) | copy-start | bytes 49156
  334.3 2.8 copy-start.2
  469.7 31.8 %copy-start.5 = (f32[48,500]{0,1:T(8,128)S(1)}, f32[48,500]{0,1:T(8,128)}, u32[]{:S(2)}) copy-start(f32[48,500]{0,1:T(8,128)} %copy-done.4) | copy-start | bytes 288004
  469.7 162.2 %copy-start.9 = (s32[48]{0:T(128)S(1)}, s32[48]{0:T(128)}, u32[]{:S(2)}) copy-start(s32[48]{0:T(128)} %param.27) | copy-start | bytes 580
  632.1 1.6 collective-permute-start
  633.7 2.4 collective-permute-start.1
  636.1 3.9 collective-permute-start.2
  640.0 2.4 collective-permute-start.3
  642.4 3.9 collective-permute-start.4
Sparse Core Ops, SparseCore 0:
  13.4 89.0 all-reduce.7
  106.6 116.7 all-reduce.5
  242.3 34.0 reduce-scatter.6
  279.0 55.3 all-gather.1
  471.1 29.4 reduce-scatter.8
